TPU v7x, 32 devices: a whole 2x2x4 slice. The times are simulated.
32 devices in a mesh: row: 4 (over y, core), col: 8 (over z, x).
Axes of the slice: x: 2, y: 2, z: 4, core: 2. Of those that a mesh axis runs over, the one named last changes fastest.
Arguments:
- tokens: bfloat16 [1024, 4096], P('row', 'col'), may hold values from -6 to 6
- gate_weight: bfloat16 [4096, 16384], P('row', 'col'), may hold values from -0.1875 to 0.1875
- up_weight: bfloat16 [4096, 16384], P('row', 'col'), may hold values from -0.1875 to 0.1875
- gate_mask: int32 [32, 128], P('row', 'col'), may hold values from 0 to 1, as said below
- up_mask: int32 [32, 128], P('row', 'col'), may hold values from 0 to 1, as said below
- cotangent: bfloat16 [1024, 16384], P('row', 'col'), may hold values from -6 to 6
Outputs:
- hidden: bfloat16 [1024, 16384], P('row', 'col')
- grad_tokens: bfloat16 [1024, 4096], P('row', 'col')
- grad_gate: bfloat16 [4096, 16384], P('row', 'col')
- grad_up: bfloat16 [4096, 16384], P('row', 'col')
Inputs may be any that keep to these rules, and one draw needn't show every extreme that they name: `gate_mask`: blocks are aligned 128 x 128 squares; each device's tile of 8 x 16 blocks keeps between 16 and 32 of them, and some tile keeps exactly 32. `up_mask`: as for gate_mask, drawn independently.
All inputs are finite; a program needn't handle non-finite values.
Results may differ from a plain program's by a relative error of at most 0.022.
Values may be sent and summed in bfloat16 or wider, within the bound.
A program may use at most 128 MiB of HBM per device.

v0:
```python
import jax
import jax.numpy as jnp
from jax import lax
from jax.sharding import PartitionSpec as P

BLK = 128


def choose_slots(flat_mask, capacity):
    position = jnp.cumsum(flat_mask, axis=-1) - 1
    slot_ids = jnp.arange(capacity, dtype=jnp.int32)
    chosen = (flat_mask[..., None, :] == 1) & (position[..., None, :] == slot_ids[:, None])
    return chosen.astype(jnp.float32)


def unpack_slots(slot_data, selector, row_blocks, col_blocks):
    shards = selector.shape[0]
    dense_blocks = jnp.einsum(
        "nsp,nsab->npab",
        selector.astype(jnp.bfloat16),
        slot_data,
        preferred_element_type=jnp.float32,
    )
    dense_blocks = dense_blocks.astype(jnp.bfloat16).reshape(
        shards, row_blocks, col_blocks, BLK, BLK
    )
    return dense_blocks.transpose(0, 1, 3, 2, 4).reshape(
        shards * row_blocks * BLK, col_blocks * BLK
    )


def masked_tile(weight, block_mask):
    expanded = jnp.repeat(jnp.repeat(block_mask, BLK, axis=0), BLK, axis=1)
    return weight * expanded.astype(jnp.bfloat16)


def pack_grads(partial_value, selector, row_blocks, col_blocks):
    shards = selector.shape[0]
    blocks = partial_value.reshape(shards, row_blocks, BLK, col_blocks, BLK).transpose(
        0, 1, 3, 2, 4
    )
    blocks = blocks.reshape(shards, row_blocks * col_blocks, BLK, BLK)
    return jnp.einsum("nsp,npab->nsab", selector, blocks, precision=lax.Precision.HIGHEST)


def body(tokens, gate_weight, up_weight, gate_mask, up_mask, cotangent):
    row_count = lax.axis_size("row")
    row_blocks, col_blocks = gate_mask.shape
    per_tile = row_blocks * col_blocks
    capacity = per_tile // 4
    gathered = lax.all_gather(tokens, "col", axis=1, tiled=True)
    gate_send = gate_mask.astype(jnp.bfloat16)
    up_send = up_mask.astype(jnp.bfloat16)
    gate_full, up_full, gate_masks, up_masks = (
        lax.all_gather(masked_tile(gate_weight, gate_mask), "row", axis=0, tiled=True),
        lax.all_gather(masked_tile(up_weight, up_mask), "row", axis=0, tiled=True),
        lax.all_gather(gate_send, "row", axis=0, tiled=True),
        lax.all_gather(up_send, "row", axis=0, tiled=True),
    )
    gate_flat = gate_masks.astype(jnp.int32).reshape(row_count, per_tile)
    up_flat = up_masks.astype(jnp.int32).reshape(row_count, per_tile)
    gate_select = choose_slots(gate_flat, capacity)
    up_select = choose_slots(up_flat, capacity)
    gate_value = jnp.dot(gathered, gate_full, preferred_element_type=jnp.float32)
    up_value = jnp.dot(gathered, up_full, preferred_element_type=jnp.float32)
    sigma = jax.nn.sigmoid(gate_value)
    hidden = (gate_value * sigma * up_value).astype(jnp.bfloat16)
    cot = cotangent.astype(jnp.float32)
    grad_gval = (cot * up_value * sigma * (1.0 + gate_value * (1.0 - sigma))).astype(jnp.bfloat16)
    grad_uval = (cot * gate_value * sigma).astype(jnp.bfloat16)
    term = jnp.dot(gate_full, grad_gval.T, preferred_element_type=jnp.float32)
    own_rows = lax.psum_scatter(
        (term + jnp.dot(up_full, grad_uval.T, preferred_element_type=jnp.float32)).astype(
            jnp.bfloat16
        ),
        "col",
        scatter_dimension=0,
        tiled=True,
    ).astype(jnp.float32)
    grad_tokens = own_rows.T.astype(jnp.bfloat16)
    contract = (((0,), (0,)), ((), ()))
    partial_g = lax.dot_general(gathered, grad_gval, contract, preferred_element_type=jnp.float32)
    partial_u = lax.dot_general(gathered, grad_uval, contract, preferred_element_type=jnp.float32)
    packed_g = pack_grads(partial_g, gate_select, row_blocks, col_blocks)
    packed_u = pack_grads(partial_u, up_select, row_blocks, col_blocks)
    summed_g, summed_u = (
        lax.psum_scatter(
            packed_g.astype(jnp.bfloat16), "row", scatter_dimension=0, tiled=True
        ).astype(jnp.float32),
        lax.psum_scatter(
            packed_u.astype(jnp.bfloat16), "row", scatter_dimension=0, tiled=True
        ).astype(jnp.float32),
    )
    own_gate = choose_slots(gate_mask.reshape(1, per_tile), capacity)
    own_up = choose_slots(up_mask.reshape(1, per_tile), capacity)
    grad_gate = unpack_slots(summed_g.astype(jnp.bfloat16), own_gate, row_blocks, col_blocks)
    grad_up = unpack_slots(summed_u.astype(jnp.bfloat16), own_up, row_blocks, col_blocks)
    return (hidden, grad_tokens, grad_gate, grad_up)


def solution(mesh):
    return jax.shard_map(
        body,
        mesh=mesh,
        in_specs=(
            P("row", "col"),
            P("row", "col"),
            P("row", "col"),
            P("row", "col"),
            P("row", "col"),
            P("row", "col"),
        ),
        out_specs=(P("row", "col"), P("row", "col"), P("row", "col"), P("row", "col")),
        check_vma=False,
    )
```

profile of v0, /device:TPU:17, one launch (start us, length us, event | category | flops | bytes accessed | tf_op | source)
XLA Modules:
  0.0 621.3 jit_solution(312473058947382219)
XLA Ops:
  7.2 0.7 all-gather.6.cloned.1.call-update
  8.0 0.8 convert_element_type.94
  8.8 4.5 broadcast_in_dim.17
  13.3 2.9 bitcast_multiply_fusion.1
  16.3 0.6 copy-done.9
  17.0 4.5 broadcast_in_dim.19
  21.5 2.9 bitcast_multiply_fusion
  24.4 0.3 reduce-scatter.4.cloned.1.call-start
  24.8 0.9 copy-done.6
  25.6 0.5 copy.19
  26.2 34.8 %all-gather.6.cloned.1.call-done = bf16[256,4096]{1,0:T(8,128)(2,1)} async-done(((bf16[256,512]{1,0:T(8,128)(2,1)}), bf16[256,4096]{1,0:T(8,128)(2,1)}) %all-gather.6.cloned.1.call-update) | async-done | bytes 2097168 | tf_op jit(solution)/shard_map/all_gather | solution.py:51
  60.9 108.0 %all-gather.4.cloned.1.call-done = bf16[4096,2048]{1,0:T(8,128)(2,1)} async-done(((bf16[1024,2048]{1,0:T(8,128)(2,1)}), bf16[4096,2048]{1,0:T(8,128)(2,1)}) %all-gather.4.cloned.1.call-update) | async-done | bytes 16777232 | tf_op jit(solution)/shard_map/all_gather | solution.py:55
  168.9 12.6 %convolution_bitcast_fusion.3 = f32[256,2048]{0,1:T(8,128)} fusion(bf16[4096,2048]{1,0:T(8,128)(2,1)} %all-gather.4.cloned.1.call-done, bf16[256,4096]{1,0:T(8,128)(2,1)} %all-gather.6.cloned.1.call-done), kind=kOutput, calls=%fused_computation.9 | convolution fusion | flops 4294967296 | bytes 20971520 | tf_op jit(solution)/shard_map/dot_general | solution.py:64
  181.5 95.5 %all-gather.8.cloned.1.call-done = bf16[4096,2048]{1,0:T(8,128)(2,1)} async-done(((bf16[1024,2048]{1,0:T(8,128)(2,1)}), bf16[4096,2048]{1,0:T(8,128)(2,1)}) %all-gather.8.cloned.1.call-update) | async-done | bytes 16777232 | tf_op jit(solution)/shard_map/all_gather | solution.py:56
  277.0 13.0 %fusion.3 = (bf16[256,2048]{0,1:T(8,128)(2,1)S(1)}, bf16[256,2048]{0,1:T(8,128)(2,1)}) fusion(bf16[256,2048]{0,1:T(8,128)(2,1)S(1)} %copy.19, f32[256,2048]{0,1:T(8,128)} %convolution_bitcast_fusion.3, bf16[4096,2048]{1,0:T(8,128)(2,1)} %all-gather.8.cloned.1.call-done, bf16[256,4096]{1,0:T(8,128)(2,1)S(1)} %copy-done), kind=kOutput, calls=%fused_computation.18 | convolution fusion | flops 4302307328 | bytes 24117248 | tf_op jit(solution)/shard_map/dot_general | solution.py:65
  290.0 1.0 copy-done.4
  291.0 9.1 %fusion.30 = f32[4096,256]{1,0:T(8,128)S(1)} fusion(bf16[4096,2048]{1,0:T(8,128)(2,1)} %all-gather.4.cloned.1.call-done, bf16[256,2048]{0,1:T(8,128)(2,1)S(1)} %get-tuple-element.12), kind=kOutput, calls=%fused_computation.55 | convolution fusion | flops 4294967296 | bytes 22020096 | tf_op jit(solution)/shard_map/dot_general | solution.py:71
  300.1 12.1 %fusion = bf16[4096,256]{1,0:T(8,128)(2,1)} fusion(f32[4096,256]{1,0:T(8,128)S(1)} %fusion.30, bf16[4096,2048]{1,0:T(8,128)(2,1)} %all-gather.8.cloned.1.call-done, f32[256,2048]{0,1:T(8,128)S(1)} %copy-done.3, bf16[256,2048]{0,1:T(8,128)(2,1)S(1)} %copy.19), kind=kOutput, calls=%fused_computation.3 | convolution fusion | flops 4300734464 | bytes 26214400 | tf_op jit(solution)/shard_map/dot_general | solution.py:73
  312.3 5.2 all_gather.19
  317.5 0.1 reshape.239
  317.6 0.3 reduce_window_sum.27
  317.9 15.2 %convolution_bitcast_fusion = f32[256,8,32,128]{3,1,2,0:T(8,128)} fusion(bf16[256,4096]{1,0:T(8,128)(2,1)S(1)} %copy-done, f32[256,2048]{0,1:T(8,128)} %convolution_bitcast_fusion.3, bf16[256,2048]{0,1:T(8,128)(2,1)S(1)} %copy.19), kind=kOutput, calls=%fused_computation | convolution fusion | flops 4298637312 | bytes 38797312 | tf_op jit(solution)/shard_map/dot_general | solution.py:83
  333.1 27.6 %copy.34 = f32[256,8,32,128]{3,2,1,0:T(8,128)} copy(f32[256,8,32,128]{3,1,2,0:T(8,128)} %convolution_bitcast_fusion) | data formatting | bytes 67108864
  360.8 58.1 %copy.24 = f32[4,8,16,128,128]{4,2,1,3,0:T(8,128)} copy(f32[4,8,16,128,128]{3,1,0,4,2:T(8,128)} %bitcast.85) | data formatting | bytes 67108864 | tf_op jit(solution)/shard_map/transpose | solution.py:39
  418.9 18.5 %convolution_convert_fusion.1 = bf16[4,32,128,128]{3,1,2,0:T(8,128)(2,1)} fusion(f32[4,128,128,128]{3,1,2,0:T(8,128)} %bitcast.83, s32[4,128]{1,0:T(4,128)S(1)} %broadcast_add_fusion, pred[4,128]{1,0:T(4,128)(4,1)S(1)} %broadcast_compare_fusion.2), kind=kOutput, calls=%fused_computation.11 | convolution fusion | flops 3223355392 | bytes 37751296 | tf_op jit(solution)/shard_map/nsp,npab->nsab/dot_general | solution.py:43
  437.4 5.2 all_gather.18
  442.6 0.1 reshape.238
  442.7 0.3 reduce_window_sum.26
  443.0 14.8 %convolution_bitcast_fusion.1 = f32[256,8,32,128]{3,1,2,0:T(8,128)} fusion(bf16[256,2048]{0,1:T(8,128)(2,1)S(1)} %copy-done.5, bf16[256,4096]{1,0:T(8,128)(2,1)S(1)} %copy-done), kind=kOutput, calls=%fused_computation.1 | convolution fusion | flops 4294967296 | bytes 36700160 | tf_op jit(solution)/shard_map/dot_general | solution.py:82
  457.8 27.6 %copy.32 = f32[256,8,32,128]{3,2,1,0:T(8,128)} copy(f32[256,8,32,128]{3,1,2,0:T(8,128)} %convolution_bitcast_fusion.1) | data formatting | bytes 67108864
  485.4 58.1 %copy.21 = f32[4,8,16,128,128]{4,2,1,3,0:T(8,128)} copy(f32[4,8,16,128,128]{3,1,0,4,2:T(8,128)} %bitcast.86) | data formatting | bytes 67108864 | tf_op jit(solution)/shard_map/transpose | solution.py:39
  543.5 18.5 %convolution_convert_fusion.3 = bf16[4,32,128,128]{3,1,2,0:T(8,128)(2,1)} fusion(f32[4,128,128,128]{3,1,2,0:T(8,128)} %bitcast.84, s32[4,128]{1,0:T(4,128)S(1)} %broadcast_add_fusion.1, pred[4,128]{1,0:T(4,128)(4,1)S(1)} %broadcast_compare_fusion.3), kind=kOutput, calls=%fused_computation.13 | convolution fusion | flops 3223355392 | bytes 37751296 | tf_op jit(solution)/shard_map/nsp,npab->nsab/dot_general | solution.py:43
  562.0 0.7 copy-done.8
  562.8 0.1 eq.99
  562.9 0.1 eq.108
  563.0 0.2 reduce-window.14
  563.2 0.2 reduce-window.15
  563.4 0.1 add_reduce_fusion.1
  563.5 0.1 add_reduce_fusion
  563.6 1.7 copy.26
  565.3 1.8 copy.27
  567.1 2.7 convolution_convert_fusion
  569.8 0.8 copy.25
  570.5 4.1 copy.40
  574.7 32.0 %reduce-scatter.6.cloned.1.call-done = bf16[1,32,128,128]{3,1,2,0:T(8,128)(2,1)} async-done(((bf16[4,32,128,128]{3,1,2,0:T(8,128)(2,1)}), bf16[1,32,128,128]{3,1,2,0:T(8,128)(2,1)}) %reduce-scatter.6.cloned.1.call-update) | async-done | bytes 1048592 | tf_op jit(solution)/shard_map/reduce_scatter | solution.py:87
  606.6 2.5 convolution_convert_fusion.2
  609.1 0.8 copy.22
  609.9 4.1 copy.41
  (43 shorter events, 0.6 us)
Async XLA Ops:
  7.2 53.8 %all-gather.6.cloned.1.call-start = ((), (), s32[]{:S(2)}) async-start(), calls=%async_computation.4 | async-start | bytes 2359296 | tf_op jit(solution)/shard_map/all_gather | solution.py:51
  7.9 161.0 %all-gather.4.cloned.1.call-start = ((), (), s32[]{:S(2)}) async-start(), calls=%async_computation.3 | async-start | bytes 20971520 | tf_op jit(solution)/shard_map/all_gather | solution.py:55
  7.9 5.4 copy-start.1
  16.3 0.7 copy-start.9
  16.3 260.7 %all-gather.8.cloned.1.call-start = ((), (), s32[]{:S(2)}) async-start(), calls=%async_computation.5 | async-start | bytes 20971520 | tf_op jit(solution)/shard_map/all_gather | solution.py:56
  16.9 4.5 copy-start.2
  24.4 1.2 copy-start.6
  24.4 540.8 %reduce-scatter.4.cloned.1.call-start = ((), (), s32[]{:S(2)}) async-start(), calls=%async_computation.6 | async-start | bytes 2359296 | tf_op jit(solution)/shard_map/reduce_scatter | solution.py:72
  60.9 216.1 %copy-start = (bf16[256,4096]{1,0:T(8,128)(2,1)S(1)}, bf16[256,4096]{1,0:T(8,128)(2,1)}, u32[]{:S(2)}) copy-start(bf16[256,4096]{1,0:T(8,128)(2,1)} %all-gather.6.cloned.1.call-done) | copy-start | bytes 6291460
  290.0 1.0 copy-start.4
  291.0 9.1 %copy-start.3 = (f32[256,2048]{0,1:T(8,128)S(1)}, f32[256,2048]{0,1:T(8,128)}, u32[]{:S(2)}) copy-start(f32[256,2048]{0,1:T(8,128)} %convolution_bitcast_fusion.3) | copy-start | bytes 6291460
  312.2 254.9 %reduce-scatter.8.cloned.1.call-start = ((), (), s32[]{:S(2)}) async-start(), calls=%async_computation.8 | async-start | bytes 5242880 | tf_op jit(solution)/shard_map/reduce_scatter | solution.py:90
  437.4 5.7 copy-start.5
  437.4 169.2 %reduce-scatter.6.cloned.1.call-start = ((), (), s32[]{:S(2)}) async-start(), calls=%async_computation.7 | async-start | bytes 5242880 | tf_op jit(solution)/shard_map/reduce_scatter | solution.py:87
  561.9 0.7 copy-start.8
  561.9 0.8 copy-start.10
  561.9 1.6 copy-start.7
Sparse Core Ops, SparseCore 0:
  10.0 50.8 all-gather.5
  63.0 105.8 all-gather.3
  171.1 105.9 all-gather.7
  312.3 64.8 reduce-scatter.3
  437.5 44.0 reduce-scatter.7
  562.1 44.5 reduce-scatter.5
where the time goes:
time: 628 us; the launch traced here: 621 us
  waiting for transfers between devices  271 us (43%)
  local copies, waits for them, and re-layouts  198 us (32%)
  matrix products  119 us (19%)
  between operations  14.7 us (2%)
  blocking collectives  10.4 us (2%)
  other arithmetic  7.93 us (1%)
    transpose x2, local copies, waits for them, and re-layouts, pack_grads(): partial_value.reshape(shards, row_blocks, BLK, col_blocks, BLK)  116 us
    all_gather x1, waiting for transfers between devices, body(): lax.all_gather(masked_tile(gate_weight, gate_mask), 'row', axis=0, tiled=...  108 us
    all_gather x1, waiting for transfers between devices, body(): lax.all_gather(masked_tile(up_weight, up_mask), 'row', axis=0, tiled=True)  95.5 us
    unnamed x29, local copies, waits for them, and re-layouts  70.6 us
    dot_general x2, matrix products, pack_grads(): jnp.einsum('nsp,npab->nsab', selector, blocks, precision=lax.Precision.HI...  37 us
    all_gather x1, waiting for transfers between devices, body(): gathered = lax.all_gather(tokens, 'col', axis=1, tiled=True)  34.8 us
    reduce_scatter x1, waiting for transfers between devices, body(): lax.psum_scatter(packed_g.astype(jnp.bfloat16), 'row', scatter_dimension=...  32 us
    dot_general x1, matrix products, body(): lax.dot_general(gathered, grad_uval, contract, preferred_element_type=jnp...  15.2 us
  transfers between devices with their start and end apart: 6, of which 4 were waited for; matrix products, arithmetic and copies ran while one was open for 45% of the time, Pallas kernels for 0%

commit v1 on v0

v1 whole, which is shorter than its diff:
```python
import functools

import jax
import jax.numpy as jnp
from jax import lax
from jax.experimental import pallas as pl
from jax.experimental.pallas import tpu as pltpu
from jax.sharding import PartitionSpec as P

BLK = 128
MESH = pl.DeviceIdType.MESH
BF = jnp.bfloat16
F32 = jnp.float32


def tables(mask, capacity):
    flat = mask.reshape(-1)
    count = flat.shape[0]
    ids = jnp.arange(count, dtype=jnp.int32)
    before = jnp.sum(jnp.where(ids[None, :] < ids[:, None], flat[None, :], 0), axis=1)
    pos = jnp.where(flat == 1, before, capacity)
    slot = jnp.arange(BLK, dtype=jnp.int32)
    place = jnp.sum(jnp.where(pos[None, :] == slot[:, None], ids[None, :], 0), axis=1)
    place = jnp.where(slot < capacity, place, 0)
    cols = mask.shape[1]
    pos = jnp.pad(pos, (0, BLK - count), constant_values=capacity)
    return pos, place // cols, place % cols


def fused(
    dims, tok, gw, uw, tab, tab_s, cot, hid, gt, pg, pu,
    wt_g, wt_u, own_g, own_u, par_g, par_u, yg, yu, fg, fu, tabs_v, tabs,
    xb, xt, gv, uv, wch, wrow, gb_g, gb_u, gtr_g, gtr_u,
    sp, rp, sy, ry, sq, rq, ow, sx, rx, sz, rz,
    ldsem, lsem, tab_ss, tab_rs, xz_s, xz_r, xp_s, xp_r, wy_s, wy_r, wp_s, wp_r, wf_s, wf_r,
    dp_s, dp_r, dy_s, dy_r, dq_s, dq_r, tx_s, tx_r, tz_s, tz_r,
):
    n_row, n_col, rb, cb, cap, nkb, toks = dims
    n_y, n_a = n_row // 2, n_col // 2
    row, col = lax.axis_index("row"), lax.axis_index("col")
    y, core = row // 2, lax.rem(row, 2)
    a, b = col // 2, lax.rem(col, 2)
    mate = y * 2 + 1 - core
    side = a * 2 + 1 - b
    pairs = cb // 2

    def y_peer(k):
        return lax.rem(y + k, n_y) * 2 + core

    def z_peer(k):
        return lax.rem(a + k, n_a) * 2 + b

    def push(src, dst, ssem, rsem, r, c):
        return pltpu.make_async_remote_copy(
            src_ref=src, dst_ref=dst, send_sem=ssem, recv_sem=rsem,
            device_id=(r, c), device_id_type=MESH,
        )

    loads = [
        [
            pltpu.make_async_copy(src.at[:, :, pl.ds(nb * BLK, BLK)], wt.at[nb], ldsem.at[m, nb])
            for nb in range(cb)
        ]
        for m, (src, wt) in enumerate(((gw, wt_g), (uw, wt_u)))
    ]
    for c in loads[0] + loads[1]:
        c.start()

    barrier = pltpu.get_barrier_semaphore()
    for k in range(1, n_row):
        pl.semaphore_signal(barrier, inc=1, device_id=(lax.rem(row + k, n_row), col), device_id_type=MESH)
    for k in range(1, n_a):
        pl.semaphore_signal(barrier, inc=1, device_id=(row, z_peer(k)), device_id_type=MESH)
    pl.semaphore_signal(barrier, inc=1, device_id=(row, side), device_id_type=MESH)
    for i in range(nkb):
        xb[col * nkb + i] = tok[:, i * BLK:(i + 1) * BLK]
    tabs_v[row] = tab[...]
    pl.semaphore_wait(barrier, n_row - 1 + n_a)

    started = []

    tab_copies = []
    for k in range(1, n_row):
        c = push(tabs_v.at[row], tabs_v.at[row], tab_ss.at[k], tab_rs.at[k], lax.rem(row + k, n_row), col)
        c.start()
        tab_copies.append(c)
    started += tab_copies

    def shard(which):
        return xb.at[pl.ds(which * nkb, nkb)]

    xz = []
    for k in range(1, n_a):
        c = push(shard(col), shard(col), xz_s.at[k], xz_r.at[k], row, z_peer(k))
        c.start()
        xz.append(c)
    xp = [push(shard(col), shard(col), xp_s.at[0], xp_r.at[0], row, side)]
    xp[0].start()

    zero = jnp.zeros((BLK, BLK), BF)
    own, par, ys, fs_ = (own_g, own_u), (par_g, par_u), (yg, yu), (fg, fu)
    for m in range(2):
        own[m][0, cap] = zero
        par[m][0, cap] = zero
        for k in range(n_y - 1):
            ys[m][k, cap] = zero
            fs_[m][k, cap] = zero

    wy = [[], []]
    wp = []
    unroll = min(8, cap)
    for m, wt in enumerate((wt_g, wt_u)):
        for c in loads[m]:
            c.wait()

        def pack(i, _, m=m, wt=wt):
            for j in range(unroll):
                s = i * unroll + j
                own[m][0, s] = wt[tab_s[3 + 2 * m, s], tab_s[2 + 2 * m, s]]
            return 0

        lax.fori_loop(0, cap // unroll, pack, 0)
        mine = own[m].at[0, pl.ds(0, cap)]
        for k in range(1, n_y):
            c = push(mine, ys[m].at[k - 1, pl.ds(0, cap)], wy_s.at[m, k], wy_r.at[m, k], y_peer(k), col)
            c.start()
            wy[m].append(c)
        c = push(mine, par[m].at[0, pl.ds(0, cap)], wp_s.at[m], wp_r.at[m], mate, col)
        c.start()
        wp.append(c)

    for c in tab_copies:
        c.wait_recv()
    to_smem = pltpu.make_async_copy(tabs_v, tabs, lsem.at[0])
    to_smem.start()
    to_smem.wait()

    for k in range(1, n_a):
        xz[k - 1].wait_recv()
        source = lax.rem(a - k + n_a, n_a) * 2 + b
        c = push(shard(source), shard(source), xp_s.at[k], xp_r.at[k], row, side)
        c.start()
        xp.append(c)
    for c in xp:
        c.wait_recv()

    def forward(ref, lead, r, m, acc, first):
        def step(i, _):
            x = jnp.concatenate([xb[r * rb + kb] for kb in range(rb)], axis=1)
            for half in range(2):
                p = i * 2 + half
                for kb in range(rb):
                    for q in range(2):
                        slot = tabs[r, m, kb * cb + p * 2 + q]
                        wch[half, kb * BLK:(kb + 1) * BLK, q * BLK:(q + 1) * BLK] = ref[lead, slot]
                d = jnp.dot(x, wch[half], preferred_element_type=F32)
                if first:
                    acc[p] = d
                else:
                    acc[p] += d
            return 0

        lax.fori_loop(0, pairs // 2, step, 0)

    accs = (gv, uv)
    for m in range(2):
        forward(own[m], 0, row, m, accs[m], True)
    for m in range(2):
        wp[m].wait_recv()
        forward(par[m], 0, mate, m, accs[m], False)

    def transpose_x(i, _):
        xt[i] = xb[i].astype(F32).T.astype(BF)
        return 0

    lax.fori_loop(0, n_row * rb, transpose_x, 0)

    wf = [[], []]
    for m in range(2):
        for k in range(1, n_y):
            wy[m][k - 1].wait_recv()
            c = push(
                ys[m].at[k - 1, pl.ds(0, cap)], fs_[m].at[k - 1, pl.ds(0, cap)],
                wf_s.at[m, k], wf_r.at[m, k], mate, col,
            )
            c.start()
            wf[m].append(c)
        for k in range(1, n_y):
            source = lax.rem(y - k + n_y, n_y) * 2
            forward(ys[m], k - 1, source + core, m, accs[m], False)
        for c in wf[m]:
            c.wait_recv()
        for k in range(1, n_y):
            source = lax.rem(y - k + n_y, n_y) * 2
            forward(fs_[m], k - 1, source + 1 - core, m, accs[m], False)

    gbs, gtrs = (gb_g, gb_u), (gtr_g, gtr_u)

    def gates(p, _):
        g, u = gv[p], uv[p]
        at = pl.ds(pl.multiple_of(p * 2 * BLK, 2 * BLK), 2 * BLK)
        c = cot[:, at].astype(F32)
        s = jax.nn.sigmoid(g)
        gs = g * s
        hid[:, at] = (gs * u).astype(BF)
        dg = (c * u * s * (1.0 + g * (1.0 - s))).astype(BF)
        du = (c * gs).astype(BF)
        for grad, blocks, turned in ((dg, gb_g, gtr_g), (du, gb_u, gtr_u)):
            blocks[p * 2] = grad[:, :BLK]
            blocks[p * 2 + 1] = grad[:, BLK:]
            turned[at, :] = grad.astype(F32).T.astype(BF)
        return 0

    lax.fori_loop(0, pairs, gates, 0)

    def weight_grad(r, m, write):
        def step(i, _):
            for j in range(unroll):
                s = i * unroll + j
                kb, nb = tabs[r, 2 + 2 * m, s], tabs[r, 3 + 2 * m, s]
                write(s, jnp.dot(xt[r * rb + kb], gbs[m][nb], preferred_element_type=F32))
            return 0

        lax.fori_loop(0, cap // unroll, step, 0)

    dp = [[], []]
    for m in range(2):
        for k in range(1, n_y):
            def write(s, v, m=m, k=k):
                sp[m, k - 1, s] = v.astype(BF)

            weight_grad(lax.rem(y + k, n_y) * 2 + 1 - core, m, write)
            c = push(sp.at[m, k - 1], rp.at[m, k - 1], dp_s.at[m, k], dp_r.at[m, k], mate, col)
            c.start()
            dp[m].append(c)
    dy = [[], []]
    for m in range(2):
        for k in range(1, n_y):
            dp[m][k - 1].wait_recv()

            def write(s, v, m=m, k=k):
                sy[m, k - 1, s] = (v + rp[m, k - 1, s].astype(F32)).astype(BF)

            weight_grad(y_peer(k), m, write)
            c = push(sy.at[m, k - 1], ry.at[m, k - 1], dy_s.at[m, k], dy_r.at[m, k], y_peer(k), col)
            c.start()
            dy[m].append(c)

    tiles = [(own, 0, row), (par, 0, mate)]
    for k in range(1, n_y):
        source = lax.rem(y - k + n_y, n_y) * 2
        tiles.append((ys, k - 1, source + core))
        tiles.append((fs_, k - 1, source + 1 - core))
    span = min(2, nkb)

    def token_grad(refs, lead, r, half, write):
        def step(i, _):
            total = None
            for m in range(2):
                for q in range(span):
                    for nb in range(cb):
                        kb = half * nkb + i * span + q
                        slot = tabs[r, m, kb * cb + nb]
                        wrow[m, q * BLK:(q + 1) * BLK, nb * BLK:(nb + 1) * BLK] = refs[m][lead, slot]
                d = jnp.dot(wrow[m], gtrs[m][...], preferred_element_type=F32)
                total = d if total is None else total + d
            write(pl.ds(pl.multiple_of(i * span * BLK, span * BLK), span * BLK), total.T)
            return 0

        lax.fori_loop(0, nkb // span, step, 0)

    tx = []
    for refs, lead, r in tiles:
        def write(at, v, r=r):
            sx[r, :, at] = v.astype(BF)

        token_grad(refs, lead, r, 1 - b, write)
    for k in range(n_a):
        at = lax.rem(a + k, n_a)
        c = push(sx.at[at], rx.at[at], tx_s.at[k], tx_r.at[k], row, side)
        c.start()
        tx.append(c)

    dq = []
    for m in range(2):
        def write(s, v, m=m):
            sq[m, s] = v.astype(BF)

        weight_grad(mate, m, write)
        c = push(sq.at[m], rq.at[m], dq_s.at[m], dq_r.at[m], mate, col)
        c.start()
        dq.append(c)

    for c in tx:
        c.wait_recv()
    for refs, lead, r in tiles:
        def write(at, v, r=r):
            sz[r, :, at] = (v + rx[r, :, at].astype(F32)).astype(BF)

        token_grad(refs, lead, r, b, write)
    tz = []
    for k in range(1, n_a):
        c = push(sz.at[lax.rem(a + k, n_a)], rz.at[k - 1], tz_s.at[k], tz_r.at[k], row, z_peer(k))
        c.start()
        tz.append(c)

    for m in range(2):
        dq[m].wait_recv()

        def write(s, v, m=m):
            ow[m, s] = (v + rq[m, s].astype(F32)).astype(BF)

        weight_grad(row, m, write)

    for c in tz:
        c.wait_recv()
    total = sz[a].astype(F32)
    for k in range(n_a - 1):
        total = total + rz[k].astype(F32)
    gt[...] = total.astype(BF)

    for m, out in enumerate((pg, pu)):
        for c in dy[m]:
            c.wait_recv()

        def finish(s, _, m=m, out=out):
            v = ow[m, s].astype(F32)
            for k in range(n_y - 1):
                v = v + ry[m, k, s].astype(F32)
            out[s] = v.astype(BF)
            return 0

        lax.fori_loop(0, cap, finish, 0)

    for group in ([*tab_copies], xz, xp, wy[0], wy[1], wp, wf[0], wf[1], dp[0], dp[1], dy[0], dy[1], dq, tx, tz):
        for c in group:
            c.wait_send()


def expand(cb, tab_s, pg, pu, grad_g, grad_u):
    i = pl.program_id(0)
    for m, (packed, out) in enumerate(((pg, grad_g), (pu, grad_u))):
        cap = packed.shape[0]
        for nb in range(cb):
            slot = tab_s[m, i * cb + nb]
            block = packed[jnp.minimum(slot, cap - 1)]
            out[:, nb * BLK:(nb + 1) * BLK] = jnp.where(slot < cap, block, jnp.zeros_like(block))


def body(n_row, n_col, tokens, gate_weight, up_weight, gate_mask, up_mask, cotangent):
    rb, cb = gate_mask.shape
    cap = rb * cb // 4
    toks, feats = tokens.shape
    nkb = feats // BLK
    units = cb * BLK
    n_y, n_a = n_row // 2, n_col // 2
    assert n_col * nkb == n_row * rb and n_a == n_row and cb % 4 == 0
    pos_g, kb_g, nb_g = tables(gate_mask, cap)
    pos_u, kb_u, nb_u = tables(up_mask, cap)
    tab = jnp.stack([pos_g, pos_u, kb_g, nb_g, kb_u, nb_u, pos_g, pos_u])

    vm = pl.BlockSpec(memory_space=pltpu.VMEM)
    anyw = pl.BlockSpec(memory_space=pl.ANY)
    sm = pl.BlockSpec(memory_space=pltpu.SMEM)
    V, D = pltpu.VMEM, pltpu.SemaphoreType.DMA
    blocks = lambda *lead: V((*lead, BLK, BLK), BF)
    scratch = [
        blocks(cb, rb), blocks(cb, rb),
        blocks(1, cap + 1), blocks(1, cap + 1), blocks(1, cap + 1), blocks(1, cap + 1),
        blocks(n_y - 1, cap + 1), blocks(n_y - 1, cap + 1),
        blocks(n_y - 1, cap + 1), blocks(n_y - 1, cap + 1),
        V((n_row, 8, BLK), jnp.int32), pltpu.SMEM((n_row, 8, BLK), jnp.int32),
        V((n_row * rb, toks, BLK), BF), V((n_row * rb, BLK, toks), BF),
        V((cb // 2, toks, 2 * BLK), F32), V((cb // 2, toks, 2 * BLK), F32),
        V((2, rb * BLK, 2 * BLK), BF), V((2, min(2, nkb) * BLK, units), BF),
        V((cb, toks, BLK), BF), V((cb, toks, BLK), BF),
        V((units, toks), BF), V((units, toks), BF),
        blocks(2, n_y - 1, cap), blocks(2, n_y - 1, cap),
        blocks(2, n_y - 1, cap), blocks(2, n_y - 1, cap),
        blocks(2, cap), blocks(2, cap), blocks(2, cap),
        V((n_a, toks, feats), BF), V((n_a, toks, feats), BF),
        V((n_a, toks, feats), BF), V((n_a - 1, toks, feats), BF),
        D((2, cb)), D((1,)), D((n_row,)), D((n_row,)), D((n_a,)), D((n_a,)), D((n_a,)), D((n_a,)),
        D((2, n_y)), D((2, n_y)), D((2,)), D((2,)), D((2, n_y)), D((2, n_y)),
        D((2, n_y)), D((2, n_y)), D((2, n_y)), D((2, n_y)), D((2,)), D((2,)),
        D((n_a,)), D((n_a,)), D((n_a,)), D((n_a,)),
    ]
    dims = (n_row, n_col, rb, cb, cap, nkb, toks)
    hidden, grad_tokens, packed_g, packed_u = pl.pallas_call(
        functools.partial(fused, dims),
        out_shape=(
            jax.ShapeDtypeStruct((toks, units), BF),
            jax.ShapeDtypeStruct((toks, feats), BF),
            jax.ShapeDtypeStruct((cap, BLK, BLK), BF),
            jax.ShapeDtypeStruct((cap, BLK, BLK), BF),
        ),
        in_specs=[vm, anyw, anyw, vm, sm, vm],
        out_specs=(vm, vm, vm, vm),
        scratch_shapes=scratch,
        compiler_params=pltpu.CompilerParams(
            collective_id=0, has_side_effects=True, vmem_limit_bytes=62 * 1024 * 1024
        ),
        name="fused_layer",
    )(
        tokens, gate_weight.reshape(rb, BLK, units), up_weight.reshape(rb, BLK, units),
        tab, tab, cotangent,
    )

    whole = lambda i: (0, 0, 0)
    grad_gate, grad_up = pl.pallas_call(
        functools.partial(expand, cb),
        grid=(rb,),
        in_specs=[
            sm,
            pl.BlockSpec((cap, BLK, BLK), whole),
            pl.BlockSpec((cap, BLK, BLK), whole),
        ],
        out_specs=(
            pl.BlockSpec((BLK, units), lambda i: (i, 0)),
            pl.BlockSpec((BLK, units), lambda i: (i, 0)),
        ),
        out_shape=(
            jax.ShapeDtypeStruct((rb * BLK, units), BF),
            jax.ShapeDtypeStruct((rb * BLK, units), BF),
        ),
        name="expand_grads",
    )(tab, packed_g, packed_u)
    return hidden, grad_tokens, grad_gate, grad_up


def solution(mesh):
    spec = P("row", "col")
    return jax.shard_map(
        functools.partial(body, mesh.shape["row"], mesh.shape["col"]),
        mesh=mesh,
        in_specs=(spec,) * 6,
        out_specs=(spec,) * 4,
        check_vma=False,
    )
```

time: 628 us -> 146 us (0.23)
  waiting for transfers between devices: 271 us -> 0 us
  local copies, waits for them, and re-layouts: 198 us -> 5.34 us
  Pallas kernels: 0 us -> 136 us
  matrix products: 119 us -> 0 us
  between operations: 14.7 us -> 0.69 us
  blocking collectives: 10.4 us -> 0 us
    all_gather x3 -> x0, waiting for transfers between devices: 238 us -> none  [the longest x1 108 us: body(): lax.all_gather(masked_tile(gate_weight, gate_mask), 'row', axis=0, tiled=...]
    pallas_call x0 -> x2, Pallas kernels: none -> 136 us  [the longest x1 129 us: body(): pl.pallas_call(functools.partial(fused, dims), out_shape=(jax.ShapeDtypeS...]
    dot_general x10 -> x0, matrix products: 119 us -> none  [the longest x2 37 us: pack_grads(): jnp.einsum('nsp,npab->nsab', selector, blocks, precision=lax.Precision.HI...]
    transpose x4 -> x0, local copies, waits for them, and re-layouts: 118 us -> none  [the longest x2 116 us: pack_grads(): partial_value.reshape(shards, row_blocks, BLK, col_blocks, BLK)]
    unnamed x29 -> x4, local copies, waits for them, and re-layouts: 70.6 us -> 3.01 us
    reduce_scatter x3 -> x0, waiting for transfers between devices: 32 us -> none  [the longest x1 32 us: body(): lax.psum_scatter(packed_g.astype(jnp.bfloat16), 'row', scatter_dimension=...]
    all_gather x2 -> x0, blocking collectives: 10.4 us -> none  [the longest x1 5.21 us: body(): lax.all_gather(up_send, 'row', axis=0, tiled=True)]
    broadcast_in_dim x4 -> x2, local copies, waits for them, and re-layouts: 9 us -> 1.54 us  [tables(): jnp.where(ids[None, :] < ids[:, None], flat[None, :], 0)]
  transfers between devices with their start and end apart: 6 -> 0, of which waited for: 4 -> 0; matrix products, arithmetic and copies ran while one was open for 45% -> 0% of each run, Pallas kernels for 0% -> 0%
where the time goes in v1:
time: 146 us; the launch traced here: 144 us
  Pallas kernels  136 us (93%)
  local copies, waits for them, and re-layouts  5.34 us (4%)
  other arithmetic  1.86 us (1%)
    pallas_call x1, Pallas kernels, body(): pl.pallas_call(functools.partial(fused, dims), out_shape=(jax.ShapeDtypeS...  129 us
    pallas_call x1, Pallas kernels, body(): pl.pallas_call(functools.partial(expand, cb), grid=(rb,), in_specs=[sm, p...  7.07 us
    unnamed x4, local copies, waits for them, and re-layouts  3.01 us

profile of v1, /device:TPU:17, one launch (start us, length us, event | category | flops | bytes accessed | tf_op | source)
XLA Modules:
  0.0 143.8 jit_solution(3278418136473126900)
XLA Ops:
  0.6 0.8 broadcast_in_dim.51
  1.4 0.1 select_reduce_fusion.3
  1.5 0.1 select_reduce_fusion.1
  1.6 0.8 broadcast_in_dim.55
  2.4 0.1 select_reduce_fusion.2
  2.5 0.1 select_reduce_fusion
  2.6 0.7 broadcast_compare_fusion.1
  3.4 0.1 eq.58
  3.4 0.7 broadcast_compare_fusion
  4.1 0.1 eq.60
  4.3 0.6 stack.2.tab.tab_s
  4.9 128.8 %fused_layer.1 = (bf16[256,2048]{1,0:T(8,128)(2,1)}, bf16[256,512]{1,0:T(8,128)(2,1)}, bf16[32,128,128]{2,1,0:T(8,128)(2,1)}, bf16[32,128,128]{2,1,0:T(8,128)(2,1)}) custom-call(bf16[256,512]{1,0:T(8,128)(2,1)} %tok.1, bf16[8,128,2048]{2,1,0:T(8,128)(2,1)} %bitcast.26, bf16[8,128,2048]{2,1,0:T(8,128)(2,1)} %bitcast.27, s32[8,128]{1,0:T(8,128)} %stack.2.tab.tab_s, ...), custom_call_target="tpu_custom_call" | custom-call | tf_op jit(solution)/shard_map/fused_layer/pallas_call | solution.py:389
  133.7 0.0 copy-start
  133.7 7.1 %expand_grads.1 = (bf16[1024,2048]{1,0:T(8,128)(2,1)}, bf16[1024,2048]{1,0:T(8,128)(2,1)}) custom-call(s32[8,128]{1,0:T(8,128)} %stack.2.tab.tab_s, bf16[32,128,128]{2,1,0:T(8,128)(2,1)} %get-tuple-element.12.pg, bf16[32,128,128]{2,1,0:T(8,128)(2,1)} %get-tuple-element.13.pu), custom_call_target="tpu_custom_call" | custom-call | tf_op jit(solution)/shard_map/expand_grads/pallas_call | solution.py:410
  140.8 2.3 %copy.12 = bf16[256,2048]{1,0:T(8,128)(2,1)} copy(bf16[256,2048]{1,0:T(8,128)(2,1)} %get-tuple-element.28) | data formatting | bytes 2097152
  143.1 0.0 copy-done
  143.1 0.7 copy.13
  (4 shorter events, 0.0 us)
Async XLA Ops:
  133.7 9.4 %copy-start = (bf16[256,512]{1,0:T(8,128)(2,1)S(1)}, bf16[256,512]{1,0:T(8,128)(2,1)}, u32[]{:S(2)}) copy-start(bf16[256,512]{1,0:T(8,128)(2,1)} %get-tuple-element.29) | copy-start | bytes 786436

commit v2 on v1

v2 whole, which is shorter than its diff:
```python
import functools

import jax
import jax.numpy as jnp
from jax import lax
from jax.experimental import pallas as pl
from jax.experimental.pallas import tpu as pltpu
from jax.sharding import PartitionSpec as P

BLK = 128
MESH = pl.DeviceIdType.MESH
BF = jnp.bfloat16
F32 = jnp.float32


def write_table(mask_ref, table, row, m, rows, cap):
    rb, cb = mask_ref.shape
    mask = mask_ref[...]
    lane = lax.broadcasted_iota(jnp.int32, (rb, BLK), 1)
    sub = lax.broadcasted_iota(jnp.int32, (rb, BLK), 0)
    sub1 = lax.broadcasted_iota(jnp.int32, (rb, 1), 0)
    cols = [mask[:, nb:nb + 1] for nb in range(cb)]
    run = jnp.zeros((rb, 1), jnp.int32)
    before = []
    for c in cols:
        before.append(run)
        run = run + c
    offset = jnp.zeros((rb, 1), jnp.int32)
    for j in range(rb):
        offset = offset + jnp.where(sub1 > j, run[j:j + 1, :], 0)
    pos = jnp.full((rb, BLK), cap, jnp.int32)
    at_kb = jnp.zeros((rb, BLK), jnp.int32)
    at_nb = jnp.zeros((rb, BLK), jnp.int32)
    for nb, c in enumerate(cols):
        slot = jnp.where(c == 1, offset + before[nb], cap)
        pos = jnp.where(lane == nb, slot, pos)
        here = (lane == slot) & (lane < cap)
        at_kb = at_kb + jnp.where(here, sub, 0)
        at_nb = at_nb + jnp.where(here, nb, 0)
    table[row, m * rows:m * rows + rb, :] = pos
    base = 2 * rows + 2 * m
    table[row, base:base + 1, :] = jnp.sum(at_kb, axis=0, keepdims=True)
    table[row, base + 1:base + 2, :] = jnp.sum(at_nb, axis=0, keepdims=True)


def fused(
    dims, tok, gw, uw, gm, um, cot, hid, gt, pg, pu, tab_out,
    wt_g, wt_u, own_g, own_u, par_g, par_u, yg, yu, fg, fu, tabs_v, tab_s, tabs,
    xb, xt, gv, uv, wch, wrow, gb_g, gb_u, gtr_g, gtr_u,
    sp, rp, sy, ry, sq, rq, ow, sx, rx, sz, rz,
    ldsem, lsem, tab_ss, tab_rs, xz_s, xz_r, xp_s, xp_r, wy_s, wy_r, wp_s, wp_r, wf_s, wf_r,
    dp_s, dp_r, dy_s, dy_r, dq_s, dq_r, tx_s, tx_r, tz_s, tz_r,
):
    n_row, n_col, rb, cb, cap, nkb, toks = dims
    n_y, n_a = n_row // 2, n_col // 2
    rows = max(8, rb)
    row, col = lax.axis_index("row"), lax.axis_index("col")
    y, core = row // 2, lax.rem(row, 2)
    a, b = col // 2, lax.rem(col, 2)
    mate = y * 2 + 1 - core
    side = a * 2 + 1 - b
    pairs = cb // 2

    def y_peer(k):
        return lax.rem(y + k, n_y) * 2 + core

    def z_peer(k):
        return lax.rem(a + k, n_a) * 2 + b

    def push(src, dst, ssem, rsem, r, c):
        return pltpu.make_async_remote_copy(
            src_ref=src, dst_ref=dst, send_sem=ssem, recv_sem=rsem,
            device_id=(r, c), device_id_type=MESH,
        )

    loads = [
        [
            pltpu.make_async_copy(src.at[:, :, pl.ds(nb * BLK, BLK)], wt.at[nb], ldsem.at[m, nb])
            for nb in range(cb)
        ]
        for m, (src, wt) in enumerate(((gw, wt_g), (uw, wt_u)))
    ]
    for c in loads[0] + loads[1]:
        c.start()

    barrier = pltpu.get_barrier_semaphore()
    for k in range(1, n_row):
        pl.semaphore_signal(barrier, inc=1, device_id=(lax.rem(row + k, n_row), col), device_id_type=MESH)
    for k in range(1, n_a):
        pl.semaphore_signal(barrier, inc=1, device_id=(row, z_peer(k)), device_id_type=MESH)
    pl.semaphore_signal(barrier, inc=1, device_id=(row, side), device_id_type=MESH)
    for i in range(nkb):
        xb[col * nkb + i] = tok[:, i * BLK:(i + 1) * BLK]
    write_table(gm, tabs_v, row, 0, rows, cap)
    write_table(um, tabs_v, row, 1, rows, cap)
    own_tab = pltpu.make_async_copy(tabs_v.at[row], tab_s, lsem.at[1])
    own_tab.start()
    tab_out[...] = tabs_v[row]
    pl.semaphore_wait(barrier, n_row - 1 + n_a)

    tab_copies = []
    for k in range(1, n_row):
        c = push(tabs_v.at[row], tabs_v.at[row], tab_ss.at[k], tab_rs.at[k], lax.rem(row + k, n_row), col)
        c.start()
        tab_copies.append(c)

    def shard(which):
        return xb.at[pl.ds(which * nkb, nkb)]

    xz = []
    for k in range(1, n_a):
        c = push(shard(col), shard(col), xz_s.at[k], xz_r.at[k], row, z_peer(k))
        c.start()
        xz.append(c)
    xp = [push(shard(col), shard(col), xp_s.at[0], xp_r.at[0], row, side)]
    xp[0].start()

    zero = jnp.zeros((BLK, BLK), BF)
    own, par, ys, fs_ = (own_g, own_u), (par_g, par_u), (yg, yu), (fg, fu)
    for m in range(2):
        own[m][0, cap] = zero
        par[m][0, cap] = zero
        for k in range(n_y - 1):
            ys[m][k, cap] = zero
            fs_[m][k, cap] = zero

    own_tab.wait()
    wy = [[], []]
    wp = []
    unroll = min(8, cap)
    for m, wt in enumerate((wt_g, wt_u)):
        for c in loads[m]:
            c.wait()

        def pack(i, _, m=m, wt=wt):
            for j in range(unroll):
                s = i * unroll + j
                own[m][0, s] = wt[tab_s[2 * rows + 2 * m + 1, s], tab_s[2 * rows + 2 * m, s]]
            return 0

        lax.fori_loop(0, cap // unroll, pack, 0)
        mine = own[m].at[0, pl.ds(0, cap)]
        for k in range(1, n_y):
            c = push(mine, ys[m].at[k - 1, pl.ds(0, cap)], wy_s.at[m, k], wy_r.at[m, k], y_peer(k), col)
            wy[m].append(c)
            if m == 0:
                c.start()
        c = push(mine, par[m].at[0, pl.ds(0, cap)], wp_s.at[m], wp_r.at[m], mate, col)
        c.start()
        wp.append(c)

    for c in tab_copies:
        c.wait_recv()
    to_smem = pltpu.make_async_copy(tabs_v, tabs, lsem.at[0])
    to_smem.start()
    to_smem.wait()

    for k in range(1, n_a):
        xz[k - 1].wait_recv()
        source = lax.rem(a - k + n_a, n_a) * 2 + b
        c = push(shard(source), shard(source), xp_s.at[k], xp_r.at[k], row, side)
        c.start()
        xp.append(c)
    for c in wy[0]:
        c.wait_send()
    for c in wy[1]:
        c.start()
    for c in xp:
        c.wait_recv()

    def forward(ref, lead, r, m, acc, first):
        def step(i, _):
            x = jnp.concatenate([xb[r * rb + kb] for kb in range(rb)], axis=1)
            for half in range(2):
                p = i * 2 + half
                for kb in range(rb):
                    for q in range(2):
                        slot = tabs[r, m * rows + kb, p * 2 + q]
                        wch[half, kb * BLK:(kb + 1) * BLK, q * BLK:(q + 1) * BLK] = ref[lead, slot]
                d = jnp.dot(x, wch[half], preferred_element_type=F32)
                if first:
                    acc[p] = d
                else:
                    acc[p] += d
            return 0

        lax.fori_loop(0, pairs // 2, step, 0)

    accs = (gv, uv)
    gbs, gtrs = (gb_g, gb_u), (gtr_g, gtr_u)

    def transpose_x(i, _):
        xt[i] = xb[i].astype(F32).T.astype(BF)
        return 0

    def near(m):
        forward(own[m], 0, row, m, accs[m], True)
        wp[m].wait_recv()
        forward(par[m], 0, mate, m, accs[m], False)

    wf = [[], []]

    def far(m):
        for k in range(1, n_y):
            wy[m][k - 1].wait_recv()
            c = push(
                ys[m].at[k - 1, pl.ds(0, cap)], fs_[m].at[k - 1, pl.ds(0, cap)],
                wf_s.at[m, k], wf_r.at[m, k], mate, col,
            )
            c.start()
            wf[m].append(c)
        for k in range(1, n_y):
            source = lax.rem(y - k + n_y, n_y) * 2
            forward(ys[m], k - 1, source + core, m, accs[m], False)
        for c in wf[m]:
            c.wait_recv()
        for k in range(1, n_y):
            source = lax.rem(y - k + n_y, n_y) * 2
            forward(fs_[m], k - 1, source + 1 - core, m, accs[m], False)

    def units(p):
        return pl.ds(pl.multiple_of(p * 2 * BLK, 2 * BLK), 2 * BLK)

    def keep(grad, p, m):
        grad = grad.astype(BF)
        gbs[m][p * 2] = grad[:, :BLK]
        gbs[m][p * 2 + 1] = grad[:, BLK:]
        gtrs[m][units(p), :] = grad.astype(F32).T.astype(BF)

    def gates_up(p, _):
        g = gv[p]
        keep(cot[:, units(p)].astype(F32) * g * jax.nn.sigmoid(g), p, 1)
        return 0

    def gates_gate(p, _):
        g, u = gv[p], uv[p]
        s = jax.nn.sigmoid(g)
        hid[:, units(p)] = (g * s * u).astype(BF)
        keep(cot[:, units(p)].astype(F32) * u * s * (1.0 + g * (1.0 - s)), p, 0)
        return 0

    def weight_grad(r, m, write):
        def step(i, _):
            for j in range(unroll):
                s = i * unroll + j
                kb, nb = tabs[r, 2 * rows + 2 * m, s], tabs[r, 2 * rows + 2 * m + 1, s]
                write(s, jnp.dot(xt[r * rb + kb], gbs[m][nb], preferred_element_type=F32))
            return 0

        lax.fori_loop(0, cap // unroll, step, 0)

    dp, dy = [[], []], [[], []]

    def far_grad_mate(m):
        for k in range(1, n_y):
            def write(s, v):
                sp[m, k - 1, s] = v.astype(BF)

            weight_grad(lax.rem(y + k, n_y) * 2 + 1 - core, m, write)
            c = push(sp.at[m, k - 1], rp.at[m, k - 1], dp_s.at[m, k], dp_r.at[m, k], mate, col)
            c.start()
            dp[m].append(c)

    def far_grad(m):
        for k in range(1, n_y):
            dp[m][k - 1].wait_recv()

            def write(s, v):
                sy[m, k - 1, s] = (v + rp[m, k - 1, s].astype(F32)).astype(BF)

            weight_grad(y_peer(k), m, write)
            c = push(sy.at[m, k - 1], ry.at[m, k - 1], dy_s.at[m, k], dy_r.at[m, k], y_peer(k), col)
            dy[m].append(c)

    near(0)
    lax.fori_loop(0, n_row * rb, transpose_x, 0)
    far(0)
    lax.fori_loop(0, pairs, gates_up, 0)
    far_grad_mate(1)
    near(1)
    far_grad(1)
    for c in wy[1]:
        c.wait_send()
    for c in dy[1]:
        c.start()
    far(1)
    lax.fori_loop(0, pairs, gates_gate, 0)
    far_grad_mate(0)

    tiles = [(own, 0, row), (par, 0, mate)]
    for k in range(1, n_y):
        source = lax.rem(y - k + n_y, n_y) * 2
        tiles.append((ys, k - 1, source + core))
        tiles.append((fs_, k - 1, source + 1 - core))
    span = min(2, nkb)

    def token_grad(refs, lead, r, half, write):
        def step(i, _):
            total = None
            for m in range(2):
                for q in range(span):
                    for nb in range(cb):
                        kb = half * nkb + i * span + q
                        slot = tabs[r, m * rows + kb, nb]
                        wrow[m, q * BLK:(q + 1) * BLK, nb * BLK:(nb + 1) * BLK] = refs[m][lead, slot]
                d = jnp.dot(wrow[m], gtrs[m][...], preferred_element_type=F32)
                total = d if total is None else total + d
            write(pl.ds(pl.multiple_of(i * span * BLK, span * BLK), span * BLK), total.T)
            return 0

        lax.fori_loop(0, nkb // span, step, 0)

    tx = []
    for i, (refs, lead, r) in enumerate(tiles):
        def write(at, v, r=r):
            sx[r, :, at] = v.astype(BF)

        token_grad(refs, lead, r, 1 - b, write)
        c = push(sx.at[r], rx.at[r], tx_s.at[i], tx_r.at[i], row, side)
        c.start()
        tx.append(c)

    far_grad(0)
    for c in dy[0]:
        c.start()

    for i, (refs, lead, r) in enumerate(tiles):
        tx[i].wait_recv()

        def write(at, v, r=r):
            sz[r, :, at] = (v + rx[r, :, at].astype(F32)).astype(BF)

        token_grad(refs, lead, r, b, write)

        @pl.when(r != a)
        def _():
            k = lax.rem(r - a + n_a, n_a)
            push(sz.at[r], rz.at[k], tz_s.at[k], tz_r.at[k], lax.axis_index("row"), r * 2 + b).start()

    dq = []
    for m in (1, 0):
        def write(s, v):
            sq[m, s] = v.astype(BF)

        weight_grad(mate, m, write)
        c = push(sq.at[m], rq.at[m], dq_s.at[m], dq_r.at[m], mate, col)
        c.start()
        dq.append(c)
    for m, c in zip((1, 0), dq):
        c.wait_recv()

        def write(s, v):
            ow[m, s] = (v + rq[m, s].astype(F32)).astype(BF)

        weight_grad(row, m, write)

    def finish(m, out):
        out[cap] = zero
        for c in dy[m]:
            c.wait_recv()

        def step(s, _):
            v = ow[m, s].astype(F32)
            for k in range(n_y - 1):
                v = v + ry[m, k, s].astype(F32)
            out[s] = v.astype(BF)
            return 0

        lax.fori_loop(0, cap, step, 0)

    finish(1, pu)
    tz = [push(sz.at[z], rz.at[k], tz_s.at[k], tz_r.at[k], row, z * 2 + b)
          for k in range(1, n_a) for z in (lax.rem(a + k, n_a),)]
    total = sz[a].astype(F32)
    for k in range(1, n_a):
        tz[k - 1].wait_recv()
        total = total + rz[k].astype(F32)
    gt[...] = total.astype(BF)
    finish(0, pg)

    for group in (tab_copies, xz, xp, wp, wf[0], wf[1], dp[0], dp[1], dy[0], dy[1], dq, tx, tz):
        for c in group:
            c.wait_send()


def expand(cb, rows, tab_s, pg, pu, hid, gt, grad_g, grad_u, hid_out, gt_out, sem):
    i = pl.program_id(0)
    copies = [
        pltpu.make_async_copy(hid, hid_out, sem.at[0]),
        pltpu.make_async_copy(gt, gt_out, sem.at[1]),
    ]

    @pl.when(i == 0)
    def _():
        for c in copies:
            c.start()

    for m, (packed, out) in enumerate(((pg, grad_g), (pu, grad_u))):
        for nb in range(cb):
            out[:, nb * BLK:(nb + 1) * BLK] = packed[tab_s[m * rows + i, nb]]

    @pl.when(i == pl.num_programs(0) - 1)
    def _():
        for c in copies:
            c.wait()


def body(n_row, n_col, tokens, gate_weight, up_weight, gate_mask, up_mask, cotangent):
    rb, cb = gate_mask.shape
    cap = rb * cb // 4
    toks, feats = tokens.shape
    nkb = feats // BLK
    units = cb * BLK
    rows = max(8, rb)
    n_y, n_a = n_row // 2, n_col // 2
    assert n_col * nkb == n_row * rb and n_a == n_row and cb % 4 == 0

    vm = pl.BlockSpec(memory_space=pltpu.VMEM)
    anyw = pl.BlockSpec(memory_space=pl.ANY)
    sm = pl.BlockSpec(memory_space=pltpu.SMEM)
    V, D = pltpu.VMEM, pltpu.SemaphoreType.DMA
    blocks = lambda *lead: V((*lead, BLK, BLK), BF)
    scratch = [
        blocks(cb, rb), blocks(cb, rb),
        blocks(1, cap + 1), blocks(1, cap + 1), blocks(1, cap + 1), blocks(1, cap + 1),
        blocks(n_y - 1, cap + 1), blocks(n_y - 1, cap + 1),
        blocks(n_y - 1, cap + 1), blocks(n_y - 1, cap + 1),
        V((n_row, 2 * rows + 8, BLK), jnp.int32),
        pltpu.SMEM((2 * rows + 8, BLK), jnp.int32), pltpu.SMEM((n_row, 2 * rows + 8, BLK), jnp.int32),
        V((n_row * rb, toks, BLK), BF), V((n_row * rb, BLK, toks), BF),
        V((cb // 2, toks, 2 * BLK), F32), V((cb // 2, toks, 2 * BLK), F32),
        V((2, rb * BLK, 2 * BLK), BF), V((2, min(2, nkb) * BLK, units), BF),
        V((cb, toks, BLK), BF), V((cb, toks, BLK), BF),
        V((units, toks), BF), V((units, toks), BF),
        blocks(2, n_y - 1, cap), blocks(2, n_y - 1, cap),
        blocks(2, n_y - 1, cap), blocks(2, n_y - 1, cap),
        blocks(2, cap), blocks(2, cap), blocks(2, cap),
        V((n_a, toks, feats), BF), V((n_a, toks, feats), BF),
        V((n_a, toks, feats), BF), V((n_a, toks, feats), BF),
        D((2, cb)), D((2,)), D((n_row,)), D((n_row,)), D((n_a,)), D((n_a,)), D((n_a,)), D((n_a,)),
        D((2, n_y)), D((2, n_y)), D((2,)), D((2,)), D((2, n_y)), D((2, n_y)),
        D((2, n_y)), D((2, n_y)), D((2, n_y)), D((2, n_y)), D((2,)), D((2,)),
        D((n_a,)), D((n_a,)), D((n_a,)), D((n_a,)),
    ]
    dims = (n_row, n_col, rb, cb, cap, nkb, toks)
    packed = jax.ShapeDtypeStruct((cap + 1, BLK, BLK), BF)
    hidden_type = jax.ShapeDtypeStruct((toks, units), BF)
    tokens_type = jax.ShapeDtypeStruct((toks, feats), BF)
    weight_type = jax.ShapeDtypeStruct((rb * BLK, units), BF)
    hidden, grad_tokens, packed_g, packed_u, tab = pl.pallas_call(
        functools.partial(fused, dims),
        out_shape=(
            hidden_type, tokens_type, packed, packed,
            jax.ShapeDtypeStruct((2 * rows + 8, BLK), jnp.int32),
        ),
        in_specs=[vm, anyw, anyw, vm, vm, vm],
        out_specs=(vm, vm, vm, vm, vm),
        scratch_shapes=scratch,
        compiler_params=pltpu.CompilerParams(
            collective_id=0, has_side_effects=True, vmem_limit_bytes=62 * 1024 * 1024
        ),
        name="fused_layer",
    )(
        tokens, gate_weight.reshape(rb, BLK, units), up_weight.reshape(rb, BLK, units),
        gate_mask, up_mask, cotangent,
    )

    whole = pl.BlockSpec((cap + 1, BLK, BLK), lambda i: (0, 0, 0))
    strip = pl.BlockSpec((BLK, units), lambda i: (i, 0))
    grad_gate, grad_up, hidden, grad_tokens = pl.pallas_call(
        functools.partial(expand, cb, rows),
        grid=(rb,),
        in_specs=[sm, whole, whole, anyw, anyw],
        out_specs=(strip, strip, anyw, anyw),
        out_shape=(weight_type, weight_type, hidden_type, tokens_type),
        scratch_shapes=[D((2,))],
        name="expand_grads",
    )(tab, packed_g, packed_u, hidden, grad_tokens)
    return hidden, grad_tokens, grad_gate, grad_up


def solution(mesh):
    spec = P("row", "col")
    return jax.shard_map(
        functools.partial(body, mesh.shape["row"], mesh.shape["col"]),
        mesh=mesh,
        in_specs=(spec,) * 6,
        out_specs=(spec,) * 4,
        check_vma=False,
    )
```

time: 146 us -> 156 us (1.068)
  Pallas kernels: 136 us -> 153 us
  local copies, waits for them, and re-layouts: 5.34 us -> 0 us
  other arithmetic: 1.86 us -> 0 us
    pallas_call x2, Pallas kernels: 136 us -> 153 us  [the longest x1 110 us: body(): pl.pallas_call(functools.partial(fused, dims), out_shape=(hidden_type, to...]
    unnamed x4 -> x0, local copies, waits for them, and re-layouts: 3.01 us -> none
where the time goes in v2:
time: 156 us; the launch traced here: 154 us
  Pallas kernels  153 us (98%)
    pallas_call x1, Pallas kernels, body(): pl.pallas_call(functools.partial(fused, dims), out_shape=(hidden_type, to...  110 us
    pallas_call x1, Pallas kernels, body(): pl.pallas_call(functools.partial(expand, cb, rows), grid=(rb,), in_specs=...  43.4 us

profile of v2, /device:TPU:17, one launch (start us, length us, event | category | flops | bytes accessed | tf_op | source)
XLA Modules:
  0.0 154.0 jit_solution(4073794779347364251)
XLA Ops:
  0.6 109.9 %fused_layer.1 = (bf16[256,2048]{1,0:T(8,128)(2,1)}, bf16[256,512]{1,0:T(8,128)(2,1)}, bf16[33,128,128]{2,1,0:T(8,128)(2,1)}, bf16[33,128,128]{2,1,0:T(8,128)(2,1)}, s32[24,128]{1,0:T(8,128)}) custom-call(bf16[256,512]{1,0:T(8,128)(2,1)} %tok.1, bf16[8,128,2048]{2,1,0:T(8,128)(2,1)} %bitcast.2, bf16[8,128,2048]{2,1,0:T(8,128)(2,1)} %bitcast.3, s32[8,16]{1,0:T(8,128)} %gm.1, ...), custom_call_target="tpu_custom_call" | custom-call | tf_op jit(solution)/shard_map/fused_layer/pallas_call | solution.py:450
  110.6 43.4 %expand_grads.1 = (bf16[1024,2048]{1,0:T(8,128)(2,1)}, bf16[1024,2048]{1,0:T(8,128)(2,1)}, bf16[256,2048]{1,0:T(8,128)(2,1)}, bf16[256,512]{1,0:T(8,128)(2,1)}) custom-call(s32[24,128]{1,0:T(8,128)} %get-tuple-element.13.tab_s, bf16[33,128,128]{2,1,0:T(8,128)(2,1)} %get-tuple-element.14.pg, bf16[33,128,128]{2,1,0:T(8,128)(2,1)} %get-tuple-element.15.pu, ...), custom_call_target="tpu_custom_call" | custom-call | tf_op jit(solution)/shard_map/expand_grads/pallas_call | solution.py:470

commit v3 on v2

--- a/solution.py
+++ b/solution.py
@@ -44,10 +44,10 @@
 
 
 def fused(
-    dims, tok, gw, uw, gm, um, cot, hid, gt, pg, pu, tab_out,
+    dims, tok, gw, uw, gm, um, cot_in, hid_out, gt, pg_out, pu_out, tab_out,
     wt_g, wt_u, own_g, own_u, par_g, par_u, yg, yu, fg, fu, tabs_v, tab_s, tabs,
     xb, xt, gv, uv, wch, wrow, gb_g, gb_u, gtr_g, gtr_u,
-    sp, rp, sy, ry, sq, rq, ow, sx, rx, sz, rz,
+    cot, hid, pg, pu, sp, rp, sy, ry, sq, rq, ow, sx, rx, sz, rz,
     ldsem, lsem, tab_ss, tab_rs, xz_s, xz_r, xp_s, xp_r, wy_s, wy_r, wp_s, wp_r, wf_s, wf_r,
     dp_s, dp_r, dy_s, dy_r, dq_s, dq_r, tx_s, tx_r, tz_s, tz_r,
 ):
@@ -80,8 +80,9 @@
         ]
         for m, (src, wt) in enumerate(((gw, wt_g), (uw, wt_u)))
     ]
-    for c in loads[0] + loads[1]:
-        c.start()
+    for c in loads[0]:
+        c.start()
+    load_cot = pltpu.make_async_copy(cot_in, cot, lsem.at[2])
 
     barrier = pltpu.get_barrier_semaphore()
     for k in range(1, n_row):
@@ -131,6 +132,11 @@
     for m, wt in enumerate((wt_g, wt_u)):
         for c in loads[m]:
             c.wait()
+        if m == 0:
+            for c in loads[1]:
+                c.start()
+        else:
+            load_cot.start()
 
         def pack(i, _, m=m, wt=wt):
             for j in range(unroll):
@@ -193,8 +199,10 @@
         xt[i] = xb[i].astype(F32).T.astype(BF)
         return 0
 
-    def near(m):
+    def near_own(m):
         forward(own[m], 0, row, m, accs[m], True)
+
+    def near_mate(m):
         wp[m].wait_recv()
         forward(par[m], 0, mate, m, accs[m], False)
 
@@ -272,19 +280,24 @@
             c = push(sy.at[m, k - 1], ry.at[m, k - 1], dy_s.at[m, k], dy_r.at[m, k], y_peer(k), col)
             dy[m].append(c)
 
-    near(0)
+    near_own(0)
+    near_mate(0)
     lax.fori_loop(0, n_row * rb, transpose_x, 0)
+    load_cot.wait()
     far(0)
     lax.fori_loop(0, pairs, gates_up, 0)
     far_grad_mate(1)
-    near(1)
+    near_own(1)
     far_grad(1)
     for c in wy[1]:
         c.wait_send()
     for c in dy[1]:
         c.start()
+    near_mate(1)
     far(1)
     lax.fori_loop(0, pairs, gates_gate, 0)
+    stores = [pltpu.make_async_copy(hid, hid_out, lsem.at[3])]
+    stores[0].start()
     far_grad_mate(0)
 
     tiles = [(own, 0, row), (par, 0, mate)]
@@ -319,10 +332,10 @@
         c = push(sx.at[r], rx.at[r], tx_s.at[i], tx_r.at[i], row, side)
         c.start()
         tx.append(c)
-
-    far_grad(0)
-    for c in dy[0]:
-        c.start()
+        if i == 0:
+            far_grad(0)
+            for c in dy[0]:
+                c.start()
 
     for i, (refs, lead, r) in enumerate(tiles):
         tx[i].wait_recv()
@@ -369,6 +382,8 @@
         lax.fori_loop(0, cap, step, 0)
 
     finish(1, pu)
+    stores.append(pltpu.make_async_copy(pu, pu_out, lsem.at[4]))
+    stores[1].start()
     tz = [push(sz.at[z], rz.at[k], tz_s.at[k], tz_r.at[k], row, z * 2 + b)
           for k in range(1, n_a) for z in (lax.rem(a + k, n_a),)]
     total = sz[a].astype(F32)
@@ -377,32 +392,23 @@
         total = total + rz[k].astype(F32)
     gt[...] = total.astype(BF)
     finish(0, pg)
+    stores.append(pltpu.make_async_copy(pg, pg_out, lsem.at[5]))
+    stores[2].start()
 
     for group in (tab_copies, xz, xp, wp, wf[0], wf[1], dp[0], dp[1], dy[0], dy[1], dq, tx, tz):
         for c in group:
             c.wait_send()
-
-
-def expand(cb, rows, tab_s, pg, pu, hid, gt, grad_g, grad_u, hid_out, gt_out, sem):
+    for c in stores:
+        c.wait()
+
+
+def expand(cb, rows, tab_s, pg, pu, hid, gt, grad_g, grad_u, hid_out, gt_out):
     i = pl.program_id(0)
-    copies = [
-        pltpu.make_async_copy(hid, hid_out, sem.at[0]),
-        pltpu.make_async_copy(gt, gt_out, sem.at[1]),
-    ]
-
-    @pl.when(i == 0)
-    def _():
-        for c in copies:
-            c.start()
-
+    hid_out[...] = hid[...]
+    gt_out[...] = gt[...]
     for m, (packed, out) in enumerate(((pg, grad_g), (pu, grad_u))):
         for nb in range(cb):
             out[:, nb * BLK:(nb + 1) * BLK] = packed[tab_s[m * rows + i, nb]]
-
-    @pl.when(i == pl.num_programs(0) - 1)
-    def _():
-        for c in copies:
-            c.wait()
 
 
 def body(n_row, n_col, tokens, gate_weight, up_weight, gate_mask, up_mask, cotangent):
@@ -432,12 +438,13 @@
         V((2, rb * BLK, 2 * BLK), BF), V((2, min(2, nkb) * BLK, units), BF),
         V((cb, toks, BLK), BF), V((cb, toks, BLK), BF),
         V((units, toks), BF), V((units, toks), BF),
+        V((toks, units), BF), V((toks, units), BF), blocks(cap + 1), blocks(cap + 1),
         blocks(2, n_y - 1, cap), blocks(2, n_y - 1, cap),
         blocks(2, n_y - 1, cap), blocks(2, n_y - 1, cap),
         blocks(2, cap), blocks(2, cap), blocks(2, cap),
         V((n_a, toks, feats), BF), V((n_a, toks, feats), BF),
         V((n_a, toks, feats), BF), V((n_a, toks, feats), BF),
-        D((2, cb)), D((2,)), D((n_row,)), D((n_row,)), D((n_a,)), D((n_a,)), D((n_a,)), D((n_a,)),
+        D((2, cb)), D((6,)), D((n_row,)), D((n_row,)), D((n_a,)), D((n_a,)), D((n_a,)), D((n_a,)),
         D((2, n_y)), D((2, n_y)), D((2,)), D((2,)), D((2, n_y)), D((2, n_y)),
         D((2, n_y)), D((2, n_y)), D((2, n_y)), D((2, n_y)), D((2,)), D((2,)),
         D((n_a,)), D((n_a,)), D((n_a,)), D((n_a,)),
@@ -453,8 +460,8 @@
             hidden_type, tokens_type, packed, packed,
             jax.ShapeDtypeStruct((2 * rows + 8, BLK), jnp.int32),
         ),
-        in_specs=[vm, anyw, anyw, vm, vm, vm],
-        out_specs=(vm, vm, vm, vm, vm),
+        in_specs=[vm, anyw, anyw, vm, vm, anyw],
+        out_specs=(anyw, vm, anyw, anyw, vm),
         scratch_shapes=scratch,
         compiler_params=pltpu.CompilerParams(
             collective_id=0, has_side_effects=True, vmem_limit_bytes=62 * 1024 * 1024
@@ -466,14 +473,15 @@
     )
 
     whole = pl.BlockSpec((cap + 1, BLK, BLK), lambda i: (0, 0, 0))
+    hid_strip = pl.BlockSpec((toks // rb, units), lambda i: (i, 0))
+    gt_strip = pl.BlockSpec((toks // rb, feats), lambda i: (i, 0))
     strip = pl.BlockSpec((BLK, units), lambda i: (i, 0))
     grad_gate, grad_up, hidden, grad_tokens = pl.pallas_call(
         functools.partial(expand, cb, rows),
         grid=(rb,),
-        in_specs=[sm, whole, whole, anyw, anyw],
-        out_specs=(strip, strip, anyw, anyw),
+        in_specs=[sm, whole, whole, hid_strip, gt_strip],
+        out_specs=(strip, strip, hid_strip, gt_strip),
         out_shape=(weight_type, weight_type, hidden_type, tokens_type),
-        scratch_shapes=[D((2,))],
         name="expand_grads",
     )(tab, packed_g, packed_u, hidden, grad_tokens)
     return hidden, grad_tokens, grad_gate, grad_up

time: 156 us -> 121 us (0.78)
  Pallas kernels: 153 us -> 118 us
    pallas_call x1, Pallas kernels: 43.4 us -> 8.09 us  [body(): pl.pallas_call(functools.partial(expand, cb, rows), grid=(rb,), in_specs=...]
where the time goes in v3:
time: 121 us; the launch traced here: 119 us
  Pallas kernels  118 us (98%)
    pallas_call x1, Pallas kernels, body(): pl.pallas_call(functools.partial(fused, dims), out_shape=(hidden_type, to...  110 us
    pallas_call x1, Pallas kernels, body(): pl.pallas_call(functools.partial(expand, cb, rows), grid=(rb,), in_specs=...  8.09 us

profile of v3, /device:TPU:17, one launch (start us, length us, event | category | flops | bytes accessed | tf_op | source)
XLA Modules:
  0.0 119.1 jit_solution(3699259725582586748)
XLA Ops:
  0.6 110.3 %fused_layer.1 = (bf16[256,2048]{1,0:T(8,128)(2,1)}, bf16[256,512]{1,0:T(8,128)(2,1)}, bf16[33,128,128]{2,1,0:T(8,128)(2,1)}, bf16[33,128,128]{2,1,0:T(8,128)(2,1)}, s32[24,128]{1,0:T(8,128)}) custom-call(bf16[256,512]{1,0:T(8,128)(2,1)} %tok.1, bf16[8,128,2048]{2,1,0:T(8,128)(2,1)} %bitcast.2, bf16[8,128,2048]{2,1,0:T(8,128)(2,1)} %bitcast.3, s32[8,16]{1,0:T(8,128)} %gm.1, ...), custom_call_target="tpu_custom_call" | custom-call | tf_op jit(solution)/shard_map/fused_layer/pallas_call | solution.py:457
  111.0 8.1 %expand_grads.1 = (bf16[1024,2048]{1,0:T(8,128)(2,1)}, bf16[1024,2048]{1,0:T(8,128)(2,1)}, bf16[256,2048]{1,0:T(8,128)(2,1)}, bf16[256,512]{1,0:T(8,128)(2,1)}) custom-call(s32[24,128]{1,0:T(8,128)} %get-tuple-element.13.tab_s, bf16[33,128,128]{2,1,0:T(8,128)(2,1)} %get-tuple-element.14.pg, bf16[33,128,128]{2,1,0:T(8,128)(2,1)} %get-tuple-element.15.pu, ...), custom_call_target="tpu_custom_call" | custom-call | tf_op jit(solution)/shard_map/expand_grads/pallas_call | solution.py:479

commit v4 on v3

--- a/solution.py
+++ b/solution.py
@@ -161,29 +161,18 @@
     to_smem.start()
     to_smem.wait()
 
-    for k in range(1, n_a):
-        xz[k - 1].wait_recv()
-        source = lax.rem(a - k + n_a, n_a) * 2 + b
-        c = push(shard(source), shard(source), xp_s.at[k], xp_r.at[k], row, side)
-        c.start()
-        xp.append(c)
-    for c in wy[0]:
-        c.wait_send()
-    for c in wy[1]:
-        c.start()
-    for c in xp:
-        c.wait_recv()
-
-    def forward(ref, lead, r, m, acc, first):
+    def forward(ref, lead, r, m, acc, first, part=None):
+        count, base = (rb, 0) if part is None else (nkb, part * nkb)
+
         def step(i, _):
-            x = jnp.concatenate([xb[r * rb + kb] for kb in range(rb)], axis=1)
+            x = jnp.concatenate([xb[r * rb + base + kb] for kb in range(count)], axis=1)
             for half in range(2):
                 p = i * 2 + half
-                for kb in range(rb):
+                for kb in range(count):
                     for q in range(2):
-                        slot = tabs[r, m * rows + kb, p * 2 + q]
+                        slot = tabs[r, m * rows + base + kb, p * 2 + q]
                         wch[half, kb * BLK:(kb + 1) * BLK, q * BLK:(q + 1) * BLK] = ref[lead, slot]
-                d = jnp.dot(x, wch[half], preferred_element_type=F32)
+                d = jnp.dot(x, wch[half, :count * BLK], preferred_element_type=F32)
                 if first:
                     acc[p] = d
                 else:
@@ -195,9 +184,12 @@
     accs = (gv, uv)
     gbs, gtrs = (gb_g, gb_u), (gtr_g, gtr_u)
 
-    def transpose_x(i, _):
-        xt[i] = xb[i].astype(F32).T.astype(BF)
-        return 0
+    def turn(which):
+        def step(i, _):
+            xt[which * nkb + i] = xb[which * nkb + i].astype(F32).T.astype(BF)
+            return 0
+
+        lax.fori_loop(0, nkb, step, 0)
 
     def near_own(m):
         forward(own[m], 0, row, m, accs[m], True)
@@ -280,9 +272,45 @@
             c = push(sy.at[m, k - 1], ry.at[m, k - 1], dy_s.at[m, k], dy_r.at[m, k], y_peer(k), col)
             dy[m].append(c)
 
-    near_own(0)
-    near_mate(0)
-    lax.fori_loop(0, n_row * rb, transpose_x, 0)
+    dq = [None, None]
+
+    def own_chip_mate(m):
+        def write(s, v):
+            sq[m, s] = v.astype(BF)
+
+        weight_grad(mate, m, write)
+        dq[m] = push(sq.at[m], rq.at[m], dq_s.at[m], dq_r.at[m], mate, col)
+        dq[m].start()
+
+    def own_chip(m):
+        dq[m].wait_recv()
+
+        def write(s, v):
+            ow[m, s] = (v + rq[m, s].astype(F32)).astype(BF)
+
+        weight_grad(row, m, write)
+
+    turn(col)
+    sources = [lax.rem(a - k + n_a, n_a) * 2 for k in range(n_a)]
+    for k in range(1, n_a):
+        xz[k - 1].wait_recv()
+        c = push(shard(sources[k] + b), shard(sources[k] + b), xp_s.at[k], xp_r.at[k], row, side)
+        c.start()
+        xp.append(c)
+    forward(own[0], 0, row, 0, gv, True, b)
+    wp[0].wait_recv()
+    forward(par[0], 0, mate, 0, gv, False, b)
+    for c in wy[0]:
+        c.wait_send()
+    for c in wy[1]:
+        c.start()
+    for k in range(1, n_a):
+        turn(sources[k] + b)
+    for k in range(n_a):
+        xp[k].wait_recv()
+        turn(sources[k] + 1 - b)
+    forward(own[0], 0, row, 0, gv, False, 1 - b)
+    forward(par[0], 0, mate, 0, gv, False, 1 - b)
     load_cot.wait()
     far(0)
     lax.fori_loop(0, pairs, gates_up, 0)
@@ -293,12 +321,18 @@
         c.wait_send()
     for c in dy[1]:
         c.start()
+    own_chip_mate(1)
     near_mate(1)
+    own_chip(1)
     far(1)
     lax.fori_loop(0, pairs, gates_gate, 0)
     stores = [pltpu.make_async_copy(hid, hid_out, lsem.at[3])]
     stores[0].start()
     far_grad_mate(0)
+    own_chip_mate(0)
+    far_grad(0)
+    for c in dy[0]:
+        c.start()
 
     tiles = [(own, 0, row), (par, 0, mate)]
     for k in range(1, n_y):
@@ -332,10 +366,6 @@
         c = push(sx.at[r], rx.at[r], tx_s.at[i], tx_r.at[i], row, side)
         c.start()
         tx.append(c)
-        if i == 0:
-            far_grad(0)
-            for c in dy[0]:
-                c.start()
 
     for i, (refs, lead, r) in enumerate(tiles):
         tx[i].wait_recv()
@@ -350,22 +380,7 @@
             k = lax.rem(r - a + n_a, n_a)
             push(sz.at[r], rz.at[k], tz_s.at[k], tz_r.at[k], lax.axis_index("row"), r * 2 + b).start()
 
-    dq = []
-    for m in (1, 0):
-        def write(s, v):
-            sq[m, s] = v.astype(BF)
-
-        weight_grad(mate, m, write)
-        c = push(sq.at[m], rq.at[m], dq_s.at[m], dq_r.at[m], mate, col)
-        c.start()
-        dq.append(c)
-    for m, c in zip((1, 0), dq):
-        c.wait_recv()
-
-        def write(s, v):
-            ow[m, s] = (v + rq[m, s].astype(F32)).astype(BF)
-
-        weight_grad(row, m, write)
+    own_chip(0)
 
     def finish(m, out):
         out[cap] = zero

time: 121 us -> 125 us (1.033); the launches traced: 119 us -> 125 us
  Pallas kernels: 118 us -> 124 us
    pallas_call x1, Pallas kernels: 110 us -> 116 us  [body(): pl.pallas_call(functools.partial(fused, dims), out_shape=(hidden_type, to...]
where the time goes in v4:
time: 125 us
  Pallas kernels  124 us (99%)
    pallas_call x1, Pallas kernels, body(): pl.pallas_call(functools.partial(fused, dims), out_shape=(hidden_type, to...  116 us
    pallas_call x1, Pallas kernels, body(): pl.pallas_call(functools.partial(expand, cb, rows), grid=(rb,), in_specs=...  8.09 us

profile of v4, /device:TPU:17, one launch (start us, length us, event | category | flops | bytes accessed | tf_op | source)
XLA Modules:
  0.0 124.6 jit_solution(13383447820447954335)
XLA Ops:
  0.6 115.8 %fused_layer.1 = (bf16[256,2048]{1,0:T(8,128)(2,1)}, bf16[256,512]{1,0:T(8,128)(2,1)}, bf16[33,128,128]{2,1,0:T(8,128)(2,1)}, bf16[33,128,128]{2,1,0:T(8,128)(2,1)}, s32[24,128]{1,0:T(8,128)}) custom-call(bf16[256,512]{1,0:T(8,128)(2,1)} %tok.1, bf16[8,128,2048]{2,1,0:T(8,128)(2,1)} %bitcast.2, bf16[8,128,2048]{2,1,0:T(8,128)(2,1)} %bitcast.3, s32[8,16]{1,0:T(8,128)} %gm.1, ...), custom_call_target="tpu_custom_call" | custom-call | tf_op jit(solution)/shard_map/fused_layer/pallas_call | solution.py:472
  116.5 8.1 %expand_grads.1 = (bf16[1024,2048]{1,0:T(8,128)(2,1)}, bf16[1024,2048]{1,0:T(8,128)(2,1)}, bf16[256,2048]{1,0:T(8,128)(2,1)}, bf16[256,512]{1,0:T(8,128)(2,1)}) custom-call(s32[24,128]{1,0:T(8,128)} %get-tuple-element.13.tab_s, bf16[33,128,128]{2,1,0:T(8,128)(2,1)} %get-tuple-element.14.pg, bf16[33,128,128]{2,1,0:T(8,128)(2,1)} %get-tuple-element.15.pu, ...), custom_call_target="tpu_custom_call" | custom-call | tf_op jit(solution)/shard_map/expand_grads/pallas_call | solution.py:494

commit v5 on v4

--- a/solution.py
+++ b/solution.py
@@ -321,18 +321,11 @@
         c.wait_send()
     for c in dy[1]:
         c.start()
-    own_chip_mate(1)
     near_mate(1)
-    own_chip(1)
     far(1)
     lax.fori_loop(0, pairs, gates_gate, 0)
     stores = [pltpu.make_async_copy(hid, hid_out, lsem.at[3])]
     stores[0].start()
-    far_grad_mate(0)
-    own_chip_mate(0)
-    far_grad(0)
-    for c in dy[0]:
-        c.start()
 
     tiles = [(own, 0, row), (par, 0, mate)]
     for k in range(1, n_y):
@@ -352,34 +345,47 @@
                         wrow[m, q * BLK:(q + 1) * BLK, nb * BLK:(nb + 1) * BLK] = refs[m][lead, slot]
                 d = jnp.dot(wrow[m], gtrs[m][...], preferred_element_type=F32)
                 total = d if total is None else total + d
-            write(pl.ds(pl.multiple_of(i * span * BLK, span * BLK), span * BLK), total.T)
+            write(i, pl.ds(pl.multiple_of(i * span * BLK, span * BLK), span * BLK), total.T)
             return 0
 
         lax.fori_loop(0, nkb // span, step, 0)
 
-    tx = []
+    pieces = [pl.ds(j * span * BLK, span * BLK) for j in range(nkb // span)]
+
+    def to_side(i, j, r, at):
+        return push(sx.at[r, :, at], rx.at[r, :, at], tx_s.at[i, j], tx_r.at[i, j], row, side)
+
+    def to_owner(k, j, z, at):
+        return push(sz.at[z, :, at], rz.at[k, :, at], tz_s.at[k, j], tz_r.at[k, j], row, z * 2 + b)
+
     for i, (refs, lead, r) in enumerate(tiles):
-        def write(at, v, r=r):
+        def write(j, at, v, i=i, r=r):
             sx[r, :, at] = v.astype(BF)
+            to_side(i, j, r, at).start()
 
         token_grad(refs, lead, r, 1 - b, write)
-        c = push(sx.at[r], rx.at[r], tx_s.at[i], tx_r.at[i], row, side)
-        c.start()
-        tx.append(c)
+        if i == 0:
+            far_grad_mate(0)
+        if i == 1:
+            far_grad(0)
+            for c in dy[0]:
+                c.start()
 
     for i, (refs, lead, r) in enumerate(tiles):
-        tx[i].wait_recv()
-
-        def write(at, v, r=r):
+        def write(j, at, v, i=i, r=r):
+            to_side(i, j, r, at).wait_recv()
             sz[r, :, at] = (v + rx[r, :, at].astype(F32)).astype(BF)
 
+            @pl.when(r != a)
+            def _():
+                to_owner(lax.rem(r - a + n_a, n_a), j, r, at).start()
+
         token_grad(refs, lead, r, b, write)
 
-        @pl.when(r != a)
-        def _():
-            k = lax.rem(r - a + n_a, n_a)
-            push(sz.at[r], rz.at[k], tz_s.at[k], tz_r.at[k], lax.axis_index("row"), r * 2 + b).start()
-
+    tx = [to_side(i, j, r, at) for i, (_, _, r) in enumerate(tiles) for j, at in enumerate(pieces)]
+    own_chip_mate(1)
+    own_chip_mate(0)
+    own_chip(1)
     own_chip(0)
 
     def finish(m, out):
@@ -399,11 +405,12 @@
     finish(1, pu)
     stores.append(pltpu.make_async_copy(pu, pu_out, lsem.at[4]))
     stores[1].start()
-    tz = [push(sz.at[z], rz.at[k], tz_s.at[k], tz_r.at[k], row, z * 2 + b)
-          for k in range(1, n_a) for z in (lax.rem(a + k, n_a),)]
+    tz = []
     total = sz[a].astype(F32)
     for k in range(1, n_a):
-        tz[k - 1].wait_recv()
+        for j, at in enumerate(pieces):
+            tz.append(to_owner(k, j, lax.rem(a + k, n_a), at))
+            tz[-1].wait_recv()
         total = total + rz[k].astype(F32)
     gt[...] = total.astype(BF)
     finish(0, pg)
@@ -462,7 +469,7 @@
         D((2, cb)), D((6,)), D((n_row,)), D((n_row,)), D((n_a,)), D((n_a,)), D((n_a,)), D((n_a,)),
         D((2, n_y)), D((2, n_y)), D((2,)), D((2,)), D((2, n_y)), D((2, n_y)),
         D((2, n_y)), D((2, n_y)), D((2, n_y)), D((2, n_y)), D((2,)), D((2,)),
-        D((n_a,)), D((n_a,)), D((n_a,)), D((n_a,)),
+        D((n_a, nkb)), D((n_a, nkb)), D((n_a, nkb)), D((n_a, nkb)),
     ]
     dims = (n_row, n_col, rb, cb, cap, nkb, toks)
     packed = jax.ShapeDtypeStruct((cap + 1, BLK, BLK), BF)

time: 125 us -> 113 us (0.904)
  Pallas kernels: 124 us -> 112 us
    pallas_call x1, Pallas kernels: 116 us -> 104 us  [body(): pl.pallas_call(functools.partial(fused, dims), out_shape=(hidden_type, to...]
where the time goes in v5:
time: 113 us
  Pallas kernels  112 us (99%)
    pallas_call x1, Pallas kernels, body(): pl.pallas_call(functools.partial(fused, dims), out_shape=(hidden_type, to...  104 us
    pallas_call x1, Pallas kernels, body(): pl.pallas_call(functools.partial(expand, cb, rows), grid=(rb,), in_specs=...  8.09 us

profile of v5, /device:TPU:17, one launch (start us, length us, event | category | flops | bytes accessed | tf_op | source)
XLA Modules:
  0.0 112.7 jit_solution(8692238848240418815)
XLA Ops:
  0.6 104.0 %fused_layer.1 = (bf16[256,2048]{1,0:T(8,128)(2,1)}, bf16[256,512]{1,0:T(8,128)(2,1)}, bf16[33,128,128]{2,1,0:T(8,128)(2,1)}, bf16[33,128,128]{2,1,0:T(8,128)(2,1)}, s32[24,128]{1,0:T(8,128)}) custom-call(bf16[256,512]{1,0:T(8,128)(2,1)} %tok.1, bf16[8,128,2048]{2,1,0:T(8,128)(2,1)} %bitcast.2, bf16[8,128,2048]{2,1,0:T(8,128)(2,1)} %bitcast.3, s32[8,16]{1,0:T(8,128)} %gm.1, ...), custom_call_target="tpu_custom_call" | custom-call | tf_op jit(solution)/shard_map/fused_layer/pallas_call | solution.py:479
  104.6 8.1 %expand_grads.1 = (bf16[1024,2048]{1,0:T(8,128)(2,1)}, bf16[1024,2048]{1,0:T(8,128)(2,1)}, bf16[256,2048]{1,0:T(8,128)(2,1)}, bf16[256,512]{1,0:T(8,128)(2,1)}) custom-call(s32[24,128]{1,0:T(8,128)} %get-tuple-element.13.tab_s, bf16[33,128,128]{2,1,0:T(8,128)(2,1)} %get-tuple-element.14.pg, bf16[33,128,128]{2,1,0:T(8,128)(2,1)} %get-tuple-element.15.pu, ...), custom_call_target="tpu_custom_call" | custom-call | tf_op jit(solution)/shard_map/expand_grads/pallas_call | solution.py:501
